TPU v7x, 256 devices: a whole 4x4x8 slice. The times are simulated.
256 devices in a mesh: ctx: 64 (over y, z, core), head: 4 (over x).
Axes of the slice: x: 4, y: 4, z: 8, core: 2. Of those that a mesh axis runs over, the one named last changes fastest.
Arguments:
- queries: bfloat16 [32768, 2048], P('ctx', 'head'), may hold values from -6 to 6
- keys: bfloat16 [32768, 2048], P('ctx', 'head'), may hold values from -6 to 6
- values: bfloat16 [32768, 2048], P('ctx', 'head'), may hold values from -6 to 6
- gain: bfloat16 [2048], P('head'), may hold values from 0.099609375 to 1.8984375
- out_weight: bfloat16 [2048, 4096], P('head', 'ctx'), may hold values from -0.125 to 0.125
- cotangent: bfloat16 [32768, 4096], P('ctx', 'head'), may hold values from -16 to 16
Outputs:
- layer_out: bfloat16 [32768, 4096], P('ctx', 'head')
- grad_queries: bfloat16 [32768, 2048], P('ctx', 'head')
- grad_keys: bfloat16 [32768, 2048], P('ctx', 'head')
- grad_values: bfloat16 [32768, 2048], P('ctx', 'head')
- grad_out_weight: float32 [2048, 4096], P('head', 'ctx')
All inputs are finite; a program needn't handle non-finite values.
Results may differ from a plain program's by a relative error of at most 0.02.
Values may be sent and summed in bfloat16 or wider, within the bound.
A program may use at most 128 MiB of HBM per device.

v0:
```python
import jax
import jax.numpy as jnp
from jax import lax
from jax.sharding import PartitionSpec as P

HDIM = 128
BLOCK = 512


EPS = 1e-06


def prefix(value, axis, combine, identity, reverse):
    count, index = (lax.axis_size(axis), lax.axis_index(axis))
    everything = lax.all_gather(value.astype(jnp.bfloat16), axis)
    start = jnp.broadcast_to(jnp.asarray(identity, value.dtype), value.shape)

    def lap(k, before):
        at = count - 1 - k if reverse else k
        reached = at > index if reverse else at < index
        new = combine(before, everything[at].astype(value.dtype))
        return jnp.where(reached, new, before)

    return lax.fori_loop(0, count, lap, start)


def on_device(queries, keys, values, gain, out_weight, cotangent):
    tok_rows, width = queries.shape
    heads = width // HDIM
    blocks = tok_rows // BLOCK
    shape_four = (blocks, BLOCK, heads, HDIM)
    q_four = queries.reshape(shape_four)
    k_four = keys.reshape(shape_four)
    v_four = values.reshape(shape_four)
    gains = gain.astype(jnp.float32).reshape(heads, HDIM)
    causal = jnp.arange(BLOCK)[:, None] >= jnp.arange(BLOCK)[None, :]
    local_states = jnp.einsum("nbhk,nbhv->nhkv", k_four, v_four, preferred_element_type=jnp.float32)
    device_state = jnp.sum(local_states, axis=0)
    zero_state = jnp.zeros_like(device_state)
    before = prefix(device_state, "ctx", jnp.add, zero_state, False)
    running = jnp.concatenate([zero_state[None], jnp.cumsum(local_states, axis=0)[:-1]], axis=0)
    prefix_state = (before[None] + running).astype(jnp.bfloat16)
    scores = jnp.einsum("nbhk,nchk->nhbc", q_four, k_four, preferred_element_type=jnp.float32)
    mixing_matrix = jnp.where(causal, scores, 0.0).astype(jnp.bfloat16)
    attended_rows = jnp.einsum(
        "nhbc,nchv->nbhv", mixing_matrix, v_four, preferred_element_type=jnp.float32
    )
    attended_rows = attended_rows + jnp.einsum(
        "nbhk,nhkv->nbhv", q_four, prefix_state, preferred_element_type=jnp.float32
    )
    scale = lax.rsqrt(jnp.mean(attended_rows * attended_rows, axis=-1, keepdims=True) + EPS)
    normed = (attended_rows * scale * gains).astype(jnp.bfloat16).reshape(tok_rows, width)
    whole_weight = lax.all_gather(out_weight, "ctx", axis=1, tiled=True)
    partial_out = jnp.dot(normed, whole_weight, preferred_element_type=jnp.float32)
    layer_out = lax.psum_scatter(
        partial_out.astype(jnp.bfloat16), "head", scatter_dimension=1, tiled=True
    )
    full_cot = lax.all_gather(cotangent, "head", axis=1, tiled=True)
    grad_normed = lax.dot_general(
        full_cot, whole_weight, (((1,), (1,)), ((), ())), preferred_element_type=jnp.float32
    )
    weight_part = lax.dot_general(
        normed, full_cot, (((0,), (0,)), ((), ())), preferred_element_type=jnp.float32
    )
    grad_out_weight = lax.psum_scatter(weight_part, "ctx", scatter_dimension=1, tiled=True)
    weighted = grad_normed.reshape(shape_four) * gains
    along = jnp.mean(weighted * attended_rows, axis=-1, keepdims=True)
    attention_gradient = (scale * weighted - scale * scale * scale * attended_rows * along).astype(
        jnp.bfloat16
    )
    local_grads = jnp.einsum(
        "nbhk,nbhv->nhkv", q_four, attention_gradient, preferred_element_type=jnp.float32
    )
    device_grad = jnp.sum(local_grads, axis=0)
    after = prefix(device_grad, "ctx", jnp.add, zero_state, True)
    inclusive = jnp.flip(jnp.cumsum(jnp.flip(local_grads, 0), axis=0), 0)
    later = jnp.concatenate([inclusive[1:], zero_state[None]], axis=0)
    suffix_state = (after[None] + later).astype(jnp.bfloat16)
    grad_scores = jnp.einsum(
        "nbhv,nchv->nhbc", attention_gradient, v_four, preferred_element_type=jnp.float32
    )
    mixing_gradient = jnp.where(causal, grad_scores, 0.0).astype(jnp.bfloat16)
    query_gradient = jnp.einsum(
        "nhbc,nchk->nbhk", mixing_gradient, k_four, preferred_element_type=jnp.float32
    )
    query_gradient = query_gradient + jnp.einsum(
        "nbhv,nhkv->nbhk", attention_gradient, prefix_state, preferred_element_type=jnp.float32
    )
    key_gradient = jnp.einsum(
        "nhbc,nbhk->nchk", mixing_gradient, q_four, preferred_element_type=jnp.float32
    )
    key_gradient = key_gradient + jnp.einsum(
        "nchv,nhkv->nchk", v_four, suffix_state, preferred_element_type=jnp.float32
    )
    value_gradient = jnp.einsum(
        "nhbc,nbhv->nchv", mixing_matrix, attention_gradient, preferred_element_type=jnp.float32
    )
    value_gradient = value_gradient + jnp.einsum(
        "nchk,nhkv->nchv", k_four, suffix_state, preferred_element_type=jnp.float32
    )
    grad_queries = query_gradient.astype(jnp.bfloat16).reshape(tok_rows, width)
    grad_keys = key_gradient.astype(jnp.bfloat16).reshape(tok_rows, width)
    grad_values = value_gradient.astype(jnp.bfloat16).reshape(tok_rows, width)
    return (layer_out, grad_queries, grad_keys, grad_values, grad_out_weight)


def solution(mesh):
    in_specs = (
        P("ctx", "head"),
        P("ctx", "head"),
        P("ctx", "head"),
        P("head"),
        P("head", "ctx"),
        P("ctx", "head"),
    )
    out_specs = (
        P("ctx", "head"),
        P("ctx", "head"),
        P("ctx", "head"),
        P("ctx", "head"),
        P("head", "ctx"),
    )
    return jax.shard_map(
        on_device, mesh=mesh, in_specs=in_specs, out_specs=out_specs, check_vma=False
    )
```

profile of v0, /device:TPU:1, one launch (start us, length us, event | category | flops | bytes accessed | tf_op | source)
XLA Modules:
  0.0 591.1 jit_solution(15734969265479801478)
XLA Ops:
  8.7 1.3 copy.98
  10.0 2.2 convolution_convert_fusion.2
  13.1 1.8 select_convert_fusion.1
  14.9 1.8 convolution_bitcast_fusion.2
  16.7 47.7 %all-gather.9.cloned.1.call-done = bf16[512,4096]{1,0:T(8,128)(2,1)} async-done(((bf16[512,1024]{1,0:T(8,128)(2,1)}), bf16[512,4096]{1,0:T(8,128)(2,1)}) %all-gather.9.cloned.1.call-update) | async-done | bytes 4194320 | tf_op jit(solution)/shard_map/all_gather | solution.py:58
  64.4 82.7 %all-gather.7.cloned.1.call-done = bf16[512,4096]{0,1:T(8,128)(2,1)} async-done(((bf16[512,64]{0,1:T(8,128)(2,1)}), bf16[512,4096]{0,1:T(8,128)(2,1)}) %all-gather.7.cloned.1.call-update) | async-done | bytes 4194320 | tf_op jit(solution)/shard_map/all_gather | solution.py:53
  147.1 6.8 %fusion.30 = f32[512,512]{0,1:T(8,128)} fusion(bf16[512,4096]{1,0:T(8,128)(2,1)} %all-gather.9.cloned.1.call-done, bf16[512,4096]{0,1:T(8,128)(2,1)} %all-gather.7.cloned.1.call-done), kind=kOutput, calls=%fused_computation.53 | convolution fusion | flops 2147483648 | bytes 9437184 | tf_op jit(solution)/shard_map/dot_general | solution.py:59
  153.9 76.9 %all-gather.11.cloned.1.call-done = bf16[256,128,128]{2,1,0:T(8,128)(2,1)} async-done(((bf16[4,128,128]{2,1,0:T(8,128)(2,1)}), bf16[256,128,128]{2,1,0:T(8,128)(2,1)}) %all-gather.11.cloned.1.call-update) | async-done | bytes 8388624 | tf_op jit(solution)/shard_map/all_gather | solution.py:15
  230.8 67.8 %while.30 = (s32[]{:T(128)}, f32[4,128,128]{2,1,0:T(8,128)S(1)}, s32[]{:T(128)}, bf16[64,4,128,128]{3,2,1,0:T(8,128)(2,1)}, s32[]{:T(128)}, /*index=5*/s32[]{:T(128)}) while((s32[]{:T(128)}, f32[4,128,128]{2,1,0:T(8,128)S(1)}, s32[]{:T(128)}, bf16[64,4,128,128]{3,2,1,0:T(8,128)(2,1)}, s32[]{:T(128)}, /*index=5*/s32[]{:T(128)}) %tuple.98), condition=%wide.region_1.2_spmd.clone, body=%wide.region_0.0_spmd.clone.sunk | while | flops 262148 | bytes 655461 | solution.py:24
  298.7 2.1 multiply_reduce_fusion
  303.1 6.5 %convolution_convert_fusion = bf16[512,4096]{1,0:T(8,128)(2,1)} fusion(bf16[512,512]{0,1:T(8,128)(2,1)S(1)} %bitcast.125, bf16[512,4096]{0,1:T(8,128)(2,1)} %all-gather.7.cloned.1.call-done), kind=kOutput, calls=%fused_computation.2 | convolution fusion | flops 2149580800 | bytes 8912896 | tf_op jit(solution)/shard_map/dot_general | solution.py:54
  310.6 2.1 select_convert_fusion
  313.6 1.1 fusion.1
  314.7 2.0 copy.48
  316.7 2.6 fusion.31
  320.2 5.7 fusion.32
  325.9 57.7 %all-gather.13.cloned.1.call-done = bf16[256,128,128]{2,1,0:T(8,128)(2,1)} async-done(((bf16[4,128,128]{2,1,0:T(8,128)(2,1)}), bf16[256,128,128]{2,1,0:T(8,128)(2,1)}) %all-gather.13.cloned.1.call-update) | async-done | bytes 8388624 | tf_op jit(solution)/shard_map/all_gather | solution.py:15
  383.6 68.3 %while.31 = (s32[]{:T(128)}, f32[4,128,128]{2,1,0:T(8,128)S(1)}, s32[]{:T(128)}, bf16[64,4,128,128]{3,2,1,0:T(8,128)(2,1)}, s32[]{:T(128)}, /*index=5*/s32[]{:T(128)}, s32[]{:T(128)}, s32[]{:T(128)}) while((s32[]{:T(128)}, f32[4,128,128]{2,1,0:T(8,128)S(1)}, s32[]{:T(128)}, bf16[64,4,128,128]{3,2,1,0:T(8,128)(2,1)}, s32[]{:T(128)}, ...), condition=%wide.region_6.7_spmd.clone, body=%wide.region_5.6_spmd.clone.sunk | while | flops 262152 | bytes 655523 | solution.py:24
  394.2 1.1 add_select_fusion.5
  395.3 1.1 add_select_fusion.5
  451.9 2.2 fusion.3
  454.1 2.1 copy.50
  456.2 1.4 fusion.2
  458.5 125.7 %reduce-scatter.5.cloned.1.call-done = f32[512,64]{0,1:T(8,128)} async-done(((f32[512,4096]{0,1:T(8,128)}), f32[512,64]{0,1:T(8,128)}) %reduce-scatter.5.cloned.1.call-update) | async-done | bytes 131088 | tf_op jit(solution)/shard_map/reduce_scatter | solution.py:65
  (180 shorter events, 139.1 us)
Async XLA Ops:
  7.2 5.9 %copy-start = (bf16[512,512]{1,0:T(8,128)(2,1)S(1)}, bf16[512,512]{1,0:T(8,128)(2,1)}, u32[]{:S(2)}) copy-start(bf16[512,512]{1,0:T(8,128)(2,1)} %param.10) | copy-start | bytes 1572868
  7.2 7.7 %copy-start.10 = (bf16[512,512]{1,0:T(8,128)(2,1)S(1)}, bf16[512,512]{1,0:T(8,128)(2,1)}, u32[]{:S(2)}) copy-start(bf16[512,512]{1,0:T(8,128)(2,1)} %param.12) | copy-start | bytes 1572868
  7.2 57.2 %all-gather.9.cloned.1.call-start = ((), (), s32[]{:S(2)}) async-start(), calls=%async_computation.4 | async-start | bytes 5242880 | tf_op jit(solution)/shard_map/all_gather | solution.py:58
  7.9 139.2 %all-gather.7.cloned.1.call-start = ((), (), s32[]{:S(2)}) async-start(), calls=%async_computation.2 | async-start | bytes 4259840 | tf_op jit(solution)/shard_map/all_gather | solution.py:53
  8.7 222.2 %all-gather.11.cloned.1.call-start = ((), (), s32[]{:S(2)}) async-start(), calls=%async_computation.6 | async-start | bytes 8519680 | tf_op jit(solution)/shard_map/all_gather | solution.py:15
  10.0 2.3 copy-start.8
  12.2 371.4 %all-gather.13.cloned.1.call-start = ((), (), s32[]{:S(2)}) async-start(), calls=%async_computation.7 | async-start | bytes 8519680 | tf_op jit(solution)/shard_map/all_gather | solution.py:15
  12.4 0.7 copy-start.13
  298.7 2.1 copy-start.7
  301.2 0.8 copy-start.3
  301.2 8.5 %copy-start.11 = (bf16[1,512,4,128]{1,3,2,0:T(8,128)(2,1)}, bf16[1,512,4,128]{1,3,2,0:T(8,128)(2,1)S(1)}, u32[]{:S(2)}) copy-start(bf16[1,512,4,128]{1,3,2,0:T(8,128)(2,1)S(1)} %get-tuple-element.259) | copy-start | bytes 1572868
  303.1 155.4 %reduce-scatter.3.cloned.1.call-start = ((), (), s32[]{:S(2)}) async-start(), calls=%async_computation.3 | async-start | bytes 5242880 | tf_op jit(solution)/shard_map/reduce_scatter | solution.py:55
  309.7 1.0 copy-start.14
  309.7 274.6 %reduce-scatter.5.cloned.1.call-start = ((), (), s32[]{:S(2)}) async-start(), calls=%async_computation.5 | async-start | bytes 8519680 | tf_op jit(solution)/shard_map/reduce_scatter | solution.py:65
  310.6 2.1 copy-start.9
  310.6 3.0 copy-start.4
  312.8 1.9 copy-start.1
  316.7 2.6 copy-start.2
  316.7 3.4 copy-start.5
  316.7 3.5 copy-start.12
  325.9 126.0 %copy-start.6 = (f32[4,128,512]{2,1,0:T(8,128)S(1)}, f32[4,128,512]{2,1,0:T(8,128)}, u32[]{:S(2)}) copy-start(f32[4,128,512]{2,1,0:T(8,128)} %fusion.31) | copy-start | bytes 3145732
Sparse Core Ops, SparseCore 0:
  9.8 54.5 all-gather.8
  67.2 79.8 all-gather.6
  150.5 80.3 all-gather.10
  303.2 80.2 all-gather.12
  386.5 46.2 reduce-scatter.2
  438.0 146.2 reduce-scatter.4
where the time goes:
time: 598 us; the launch traced here: 591 us
  waiting for transfers between devices  392 us (66%)
  other arithmetic  134 us (22%)
  matrix products  37.9 us (6%)
  between operations  14.3 us (2%)
  local copies, waits for them, and re-layouts  8.98 us (2%)
    all_gather x2, waiting for transfers between devices, prefix(): everything = lax.all_gather(value.astype(jnp.bfloat16), axis)  135 us
    select_n x128, other arithmetic, lap(): return jnp.where(reached, new, before)  133 us
    reduce_scatter x1, waiting for transfers between devices, on_device(): lax.psum_scatter(weight_part, 'ctx', scatter_dimension=1, tiled=True)  126 us
    all_gather x1, waiting for transfers between devices, on_device(): whole_weight = lax.all_gather(out_weight, 'ctx', axis=1, tiled=True)  82.7 us
    all_gather x1, waiting for transfers between devices, on_device(): full_cot = lax.all_gather(cotangent, 'head', axis=1, tiled=True)  47.7 us
  transfers between devices with their start and end apart: 6, of which 5 were waited for; matrix products, arithmetic and copies ran while one was open for 18% of the time, Pallas kernels for 0%

commit v1 on v0

v1 whole, which is shorter than its diff:
```python
import jax
import jax.numpy as jnp
from jax import lax
from jax.experimental import pallas as pl
from jax.experimental.pallas import tpu as pltpu
from jax.sharding import PartitionSpec as P

HDIM = 128
HEADS = 4
ROWS = 512
NX, NY, NZ = 4, 4, 8
GROUP = 2 * NZ
SLICE = HEADS * HDIM // GROUP
PIECE = 64
EPS = 1e-06
MESH = pl.DeviceIdType.MESH
F32, BF16 = jnp.float32, jnp.bfloat16


def dot(a, b, ca, cb):
    return lax.dot_general(a, b, (((ca,), (cb,)), ((), ())), preferred_element_type=F32)


def copy_to(src, dst, send_sem, recv_sem, device):
    return pltpu.make_async_remote_copy(
        src_ref=src, dst_ref=dst, send_sem=send_sem, recv_sem=recv_sem,
        device_id=device, device_id_type=MESH,
    )


def head(h):
    return slice(h * HDIM, (h + 1) * HDIM)


def kernel(
    q_ref, k_ref, v_ref, g_ref, w_ref, c_ref,
    out_ref, gq_ref, gk_ref, gv_ref, gw_ref,
    wt, state, slices, partial, totals, back, states,
    att, inv, normed, cot_t, gn_stage, gn_recv, gn_own, ga,
    pair_stage, pair_recv, dsum, ring_stage, ring_recv, last_stage, last_recv,
    w0_send, w0_recv, wz_send, wz_recv, wc_send, wc_recv,
    s1_send, s1_recv, s2_send, s2_recv, s3_send, s3_recv,
    n_send, n_recv, gn_send, gn_rsem, pair_send, pair_rsem,
    ring_send, ring_rsem, last_send, last_rsem,
):
    ctx, x = lax.axis_index("ctx"), lax.axis_index("head")
    y, z, core = ctx // GROUP, (ctx // 2) % NZ, ctx % 2
    g = ctx % GROUP
    me_diag = x == y

    def dev(x, y, z, core):
        return (y * GROUP + z * 2 + core, x)

    step = 1 - 2 * core
    z_major, z_minor = (z + step + NZ) % NZ, (z - step + NZ) % NZ
    x_major, x_minor, x_opp = (x + step + NX) % NX, (x - step + NX) % NX, (x + 2) % NX
    d_major, d_minor = dev(x, y, z_major, core), dev(x, y, z_minor, core)
    e_major, e_minor = dev(x_major, y, z, core), dev(x_minor, y, z, core)
    sibling = dev(x, y, z, 1 - core)
    sent = []

    def send(*args):
        c = copy_to(*args)
        c.start()
        sent.append(c)

    barrier = pltpu.get_barrier_semaphore()

    def hello(device):
        pl.semaphore_signal(barrier, inc=1, device_id=device, device_id_type=MESH)

    def hello_group(d, carry):
        hello((y * GROUP + (g + d) % GROUP, x))
        return carry

    lax.fori_loop(1, GROUP, hello_group, 0)
    for d in range(1, NY):
        hello(dev(x, (y + d) % NY, z, core))
    hello(e_major)
    hello(e_minor)
    for j in range(NX):
        for there in ((y, j), (j, x)):
            @pl.when(jnp.logical_or(there[0] != x, there[1] != y))
            def _():
                hello(dev(there[0], there[1], z, core))
    pl.semaphore_wait(barrier, (GROUP - 1) + (NY - 1) + 2 + 2 * NX - 2 * me_diag.astype(jnp.int32))

    for j in range(NY):
        away = jnp.logical_or(y != x, j != y)

        @pl.when(away)
        def _():
            copy_to(w_ref, wt.at[z, core, x], w0_send.at[j], w0_recv.at[x], dev(y, j, z, core)).start()

        @pl.when(jnp.logical_not(away))
        def _():
            wt[z, core, x] = w_ref[...]

    def scan_start(way):
        for h in range(HEADS):
            state[way, h * (HDIM // SLICE):(h + 1) * (HDIM // SLICE)] = (
                scan_term(way, h).astype(BF16).reshape(HDIM // SLICE, SLICE, HDIM)
            )

        def go(d, carry):
            to = (g + d) % GROUP
            copy_to(state.at[way, to], slices.at[way, g], s1_send.at[way, d], s1_recv.at[way, g],
                    (y * GROUP + to, x)).start()
            return carry

        lax.fori_loop(1, GROUP, go, 0)
        slices[way, g] = state[way, g]

    def scan_term(way, h):
        if way == 0:
            return dot(k_ref[:, head(h)], v_ref[:, head(h)], 0, 0)
        return dot(q_ref[:, head(h)], ga[:, head(h)], 0, 0)

    def scan_totals(way):
        def arrive(d, carry):
            at = (g + d) % GROUP
            copy_to(slices.at[way, at], slices.at[way, at], s1_send.at[way, d], s1_recv.at[way, at], sibling).wait_recv()
            return carry

        lax.fori_loop(1, GROUP, arrive, 0)
        run = jnp.zeros((SLICE, HDIM), F32)
        for i in (range(GROUP) if way == 0 else range(GROUP - 1, -1, -1)):
            partial[way, i] = run
            run = run + slices[way, i].astype(F32)
        totals[way, y] = run
        for d in range(1, NY):
            send(totals.at[way, y], totals.at[way, y], s2_send.at[way, d], s2_recv.at[way, y],
                 dev(x, (y + d) % NY, z, core))

    def scan_back(way):
        for d in range(1, NY):
            at = (y + d) % NY
            copy_to(totals.at[way, at], totals.at[way, at], s2_send.at[way, d], s2_recv.at[way, at], sibling).wait_recv()
        offset = jnp.zeros((SLICE, HDIM), F32)
        for j in range(NY):
            counts = (j < y) if way == 0 else (j > y)
            offset = offset + jnp.where(counts, totals[way, j], 0.0)
        for i in range(GROUP):
            back[way, i] = (partial[way, i] + offset).astype(BF16)

        def go(d, carry):
            to = (g + d) % GROUP
            copy_to(back.at[way, to], states.at[way, g], s3_send.at[way, d], s3_recv.at[way, g],
                    (y * GROUP + to, x)).start()
            return carry

        lax.fori_loop(1, GROUP, go, 0)
        states[way, g] = back[way, g]

    def scan_end(way):
        def arrive(d, carry):
            at = (g + d) % GROUP
            copy_to(states.at[way, at], states.at[way, at], s3_send.at[way, d], s3_recv.at[way, at], sibling).wait_recv()
            return carry

        lax.fori_loop(1, GROUP, arrive, 0)

    def state_of(way, h):
        n = HDIM // SLICE
        return states[way, h * n:(h + 1) * n].reshape(HDIM, HDIM)

    scan_start(0)

    def to_sibling(i, at):
        send(wt.at[at, core], wt.at[at, core], wc_send.at[i], wc_recv.at[i], sibling)

    def w_first():
        for a in range(NX):
            @pl.when(jnp.logical_or(y != x, a != x))
            def _():
                copy_to(wt.at[z, core, a], wt.at[z, core, a], w0_send.at[a], w0_recv.at[a], sibling).wait_recv()
        send(wt.at[z, core], wt.at[z, core], wz_send.at[0], wz_recv.at[0], d_major)
        send(wt.at[z, core], wt.at[z, core], wz_send.at[4], wz_recv.at[4], d_minor)
        to_sibling(0, z)

    def w_wait(i, at):
        copy_to(wt.at[at, core], wt.at[at, core], wz_send.at[i], wz_recv.at[i], sibling).wait_recv()

    def w_step(s):
        at = (z - step * s + NZ) % NZ
        w_wait(s - 1, at)
        if s < 4:
            send(wt.at[at, core], wt.at[at, core], wz_send.at[s], wz_recv.at[s], d_major)
        to_sibling(s, at)
        if s < 4:
            at = (z + step * s + NZ) % NZ
            w_wait(3 + s, at)
            if s < 3:
                send(wt.at[at, core], wt.at[at, core], wz_send.at[4 + s], wz_recv.at[4 + s], d_minor)
            to_sibling(4 + s, at)

    def w_end():
        for s in range(8):
            at = (z - step * (s - 4) + NZ) % NZ if s > 4 else (z + step * s + NZ) % NZ
            copy_to(wt.at[at, 1 - core], wt.at[at, 1 - core], wc_send.at[s], wc_recv.at[s], sibling).wait_recv()

    row = lax.broadcasted_iota(jnp.int32, (ROWS, ROWS), 0)
    col = lax.broadcasted_iota(jnp.int32, (ROWS, ROWS), 1)

    def local_attention(h):
        s = dot(q_ref[:, head(h)], k_ref[:, head(h)], 1, 1)
        m = jnp.where(row >= col, s, 0.0).astype(BF16)
        att[:, head(h)] = dot(m, v_ref[:, head(h)], 1, 0)

    w_first()
    local_attention(0)
    local_attention(1)
    scan_totals(0)
    w_step(1)
    local_attention(2)
    local_attention(3)
    scan_back(0)
    w_step(2)
    cot_t[...] = c_ref[...].T.reshape(NZ, 2, PIECE, ROWS)
    scan_end(0)

    gain = g_ref[...].astype(F32)
    for h in range(HEADS):
        a = att[:, head(h)] + dot(q_ref[:, head(h)], state_of(0, h), 1, 0)
        scale = lax.rsqrt(jnp.mean(a * a, axis=-1, keepdims=True) + EPS)
        a = a * scale
        att[:, head(h)] = a
        inv[h] = scale
        normed[x, :, head(h)] = (a * gain[:, head(h)]).astype(BF16)
    send(normed.at[x], normed.at[x], n_send.at[0], n_recv.at[0], e_major)
    send(normed.at[x], normed.at[x], n_send.at[1], n_recv.at[1], e_minor)
    w_step(3)

    def n_wait(i, at):
        copy_to(normed.at[at], normed.at[at], n_send.at[i], n_recv.at[i], sibling).wait_recv()

    def pair_go(p, a):
        other = cot_t[:, 1 - core].reshape(ROWS, ROWS)
        pair_stage[p] = dot(other, normed[a], 1, 0).astype(BF16).reshape(NZ, PIECE, ROWS)
        send(pair_stage.at[p], pair_recv.at[p], pair_send.at[p], pair_rsem.at[p], sibling)
        mine = cot_t[:, core].reshape(ROWS, ROWS)
        dsum[p] = dot(mine, normed[a], 1, 0).reshape(NZ, PIECE, ROWS)

    def pair_end(p):
        copy_to(pair_stage.at[p], pair_recv.at[p], pair_send.at[p], pair_rsem.at[p], sibling).wait_recv()
        dsum[p] = dsum[p] + pair_recv[p].astype(F32)

    def ring_wait(p, i):
        copy_to(ring_stage.at[p, i], ring_recv.at[p, i], ring_send.at[p, i], ring_rsem.at[p, i], sibling).wait_recv()

    def ring_step(p, s):
        at = (z + step * (4 - s) + NZ) % NZ
        term = dsum[p, at]
        if s:
            ring_wait(p, s - 1)
            term = term + ring_recv[p, s - 1].astype(F32)
        ring_stage[p, s] = term.astype(BF16)
        send(ring_stage.at[p, s], ring_recv.at[p, s], ring_send.at[p, s], ring_rsem.at[p, s], d_major)
        if s < 3:
            at = (z - step * (3 - s) + NZ) % NZ
            term = dsum[p, at]
            if s:
                ring_wait(p, 3 + s)
                term = term + ring_recv[p, 3 + s].astype(F32)
            i = 4 + s
            ring_stage[p, i] = term.astype(BF16)
            send(ring_stage.at[p, i], ring_recv.at[p, i], ring_send.at[p, i], ring_rsem.at[p, i], d_minor)

    def ring_end(p, a):
        ring_wait(p, 3)
        ring_wait(p, 6)
        total = dsum[p, z] + ring_recv[p, 3].astype(F32) + ring_recv[p, 6].astype(F32)
        last_stage[p] = total.astype(BF16)
        away = jnp.logical_or(a != x, x != y)

        @pl.when(away)
        def _():
            copy_to(last_stage.at[p], last_recv.at[y], last_send.at[p], last_rsem.at[y], dev(a, x, z, core)).start()

        @pl.when(jnp.logical_not(away))
        def _():
            last_recv[y] = last_stage[p]

    quarters = (x, (x + 3) % NX, (x + 1) % NX, x_opp)

    def ring_all(p):
        pair_end(p)
        for s in range(4):
            ring_step(p, s)

    def gn_part(a):
        w = wt[:, :, a].reshape(NZ * 2 * PIECE, ROWS)
        return dot(c_ref[...], w, 1, 0)

    def gn_wait(i):
        copy_to(gn_stage.at[i], gn_recv.at[i], gn_send.at[i], gn_rsem.at[i], sibling).wait_recv()

    pair_go(0, quarters[0])
    w_step(4)
    w_end()
    gn_stage[0] = gn_part(x_opp).astype(BF16)
    send(gn_stage.at[0], gn_recv.at[0], gn_send.at[0], gn_rsem.at[0], e_major)
    n_wait(0, x_minor)
    send(normed.at[x_minor], normed.at[x_minor], n_send.at[2], n_recv.at[2], e_major)
    gn_stage[1] = gn_part(x_minor).astype(BF16)
    send(gn_stage.at[1], gn_recv.at[1], gn_send.at[1], gn_rsem.at[1], e_minor)
    ring_all(0)
    n_wait(1, x_major)
    pair_go(1, quarters[1])
    pair_go(2, quarters[2])
    gn_wait(0)
    gn_stage[2] = (gn_part(x_major) + gn_recv[0].astype(F32)).astype(BF16)
    send(gn_stage.at[2], gn_recv.at[2], gn_send.at[2], gn_rsem.at[2], e_major)
    gn_own[...] = gn_part(x)
    pair_end(1)
    pair_end(2)
    for s in range(4):
        ring_step(1, s)
        ring_step(2, s)
    n_wait(2, x_opp)
    pair_go(3, quarters[3])
    ring_all(3)
    for p in range(3):
        ring_end(p, quarters[p])

    gn_wait(1)
    gn_wait(2)
    for h in range(HEADS):
        w = gn_own[:, head(h)] + gn_recv[1, :, head(h)].astype(F32) + gn_recv[2, :, head(h)].astype(F32)
        w = w * gain[:, head(h)]
        a = att[:, head(h)]
        along = jnp.mean(w * a, axis=-1, keepdims=True)
        ga[:, head(h)] = (inv[h] * (w - a * along)).astype(BF16)
    scan_start(1)
    ring_end(3, quarters[3])

    def queries_gradient(h):
        s = dot(ga[:, head(h)], v_ref[:, head(h)], 1, 1)
        m = jnp.where(row >= col, s, 0.0).astype(BF16)
        t = dot(m, k_ref[:, head(h)], 1, 0) + dot(ga[:, head(h)], state_of(0, h), 1, 1)
        gq_ref[:, head(h)] = t.astype(BF16)

    def local_keys_values(h):
        s = dot(v_ref[:, head(h)], ga[:, head(h)], 1, 1)
        m = jnp.where(col >= row, s, 0.0).astype(BF16)
        gn_own[:, head(h)] = dot(m, q_ref[:, head(h)], 1, 0)
        s = dot(k_ref[:, head(h)], q_ref[:, head(h)], 1, 1)
        m = jnp.where(col >= row, s, 0.0).astype(BF16)
        att[:, head(h)] = dot(m, ga[:, head(h)], 1, 0)

    for h in range(HEADS):
        queries_gradient(h)
    scan_totals(1)
    for h in range(HEADS):
        local_keys_values(h)
    scan_back(1)

    def out_rows(i, carry):
        r = pl.ds(pl.multiple_of(i * 128, 128), 128)
        total = jnp.zeros((128, NZ * 2 * PIECE), F32)
        for a in range(NX):
            w = wt[:, :, a].reshape(NZ * 2 * PIECE, ROWS)
            total = total + dot(normed[a, r, :], w, 1, 1)
        out_ref[r, :] = total.astype(BF16)
        return carry

    lax.fori_loop(0, ROWS // 128, out_rows, 0)

    scan_end(1)
    for h in range(HEADS):
        st = state_of(1, h)
        gk_ref[:, head(h)] = (gn_own[:, head(h)] + dot(v_ref[:, head(h)], st, 1, 1)).astype(BF16)
        gv_ref[:, head(h)] = (att[:, head(h)] + dot(k_ref[:, head(h)], st, 1, 0)).astype(BF16)

    for j in range(NY):
        @pl.when(jnp.logical_or(y != x, j != y))
        def _():
            copy_to(last_stage.at[0], last_recv.at[j], last_send.at[0], last_rsem.at[j], sibling).wait_recv()
    gw_ref[...] = (
        (last_recv[0].astype(F32) + last_recv[1].astype(F32))
        + (last_recv[2].astype(F32) + last_recv[3].astype(F32))
    )

    for c in sent:
        c.wait_send()
    for j in range(NY):
        @pl.when(jnp.logical_or(y != x, j != y))
        def _():
            copy_to(w_ref, wt.at[z, core, x], w0_send.at[j], w0_recv.at[x], sibling).wait_send()
    for p in range(NX):
        @pl.when(jnp.logical_or(quarters[p] != x, y != x))
        def _():
            copy_to(last_stage.at[p], last_recv.at[y], last_send.at[p], last_rsem.at[y], sibling).wait_send()

    def left(d, carry):
        for way in range(2):
            to = (g + d) % GROUP
            copy_to(state.at[way, to], slices.at[way, g], s1_send.at[way, d], s1_recv.at[way, g], sibling).wait_send()
            copy_to(back.at[way, to], states.at[way, g], s3_send.at[way, d], s3_recv.at[way, g], sibling).wait_send()
        return carry

    lax.fori_loop(1, GROUP, left, 0)


def on_device(queries, keys, values, gain, out_weight, cotangent):
    width = HEADS * HDIM
    cols = NZ * 2 * PIECE
    vmem = pl.BlockSpec(memory_space=pltpu.VMEM)
    dma = pltpu.SemaphoreType.DMA
    outs = pl.pallas_call(
        kernel,
        out_shape=(
            jax.ShapeDtypeStruct((ROWS, cols), BF16),
            jax.ShapeDtypeStruct((ROWS, width), BF16),
            jax.ShapeDtypeStruct((ROWS, width), BF16),
            jax.ShapeDtypeStruct((ROWS, width), BF16),
            jax.ShapeDtypeStruct((PIECE, width), F32),
        ),
        in_specs=[vmem] * 6,
        out_specs=(vmem,) * 5,
        scratch_shapes=[
            pltpu.VMEM((NZ, 2, NX, PIECE, width), BF16),
            pltpu.VMEM((2, GROUP, SLICE, HDIM), BF16),
            pltpu.VMEM((2, GROUP, SLICE, HDIM), BF16),
            pltpu.VMEM((2, GROUP, SLICE, HDIM), F32),
            pltpu.VMEM((2, NY, SLICE, HDIM), F32),
            pltpu.VMEM((2, GROUP, SLICE, HDIM), BF16),
            pltpu.VMEM((2, GROUP, SLICE, HDIM), BF16),
            pltpu.VMEM((ROWS, width), F32),
            pltpu.VMEM((HEADS, ROWS, 1), F32),
            pltpu.VMEM((NX, ROWS, width), BF16),
            pltpu.VMEM((NZ, 2, PIECE, ROWS), BF16),
            pltpu.VMEM((3, ROWS, width), BF16),
            pltpu.VMEM((3, ROWS, width), BF16),
            pltpu.VMEM((ROWS, width), F32),
            pltpu.VMEM((ROWS, width), BF16),
            pltpu.VMEM((NX, NZ, PIECE, width), BF16),
            pltpu.VMEM((NX, NZ, PIECE, width), BF16),
            pltpu.VMEM((NX, NZ, PIECE, width), F32),
            pltpu.VMEM((NX, 7, PIECE, width), BF16),
            pltpu.VMEM((NX, 7, PIECE, width), BF16),
            pltpu.VMEM((NX, PIECE, width), BF16),
            pltpu.VMEM((NY, PIECE, width), BF16),
            dma((NY,)), dma((NX,)), dma((7,)), dma((7,)), dma((8,)), dma((8,)),
            dma((2, GROUP)), dma((2, GROUP)), dma((2, NY)), dma((2, NY)), dma((2, GROUP)), dma((2, GROUP)),
            dma((3,)), dma((3,)), dma((3,)), dma((3,)), dma((NX,)), dma((NX,)),
            dma((NX, 7)), dma((NX, 7)), dma((NX,)), dma((NY,)),
        ],
        compiler_params=pltpu.CompilerParams(
            collective_id=0, has_side_effects=True, vmem_limit_bytes=56 * 1024 * 1024
        ),
    )(queries, keys, values, gain.reshape(1, width), out_weight.T, cotangent)
    return outs[:4] + (outs[4].T,)


def solution(mesh):
    in_specs = (
        P("ctx", "head"),
        P("ctx", "head"),
        P("ctx", "head"),
        P("head"),
        P("head", "ctx"),
        P("ctx", "head"),
    )
    out_specs = (
        P("ctx", "head"),
        P("ctx", "head"),
        P("ctx", "head"),
        P("ctx", "head"),
        P("head", "ctx"),
    )
    return jax.shard_map(
        on_device, mesh=mesh, in_specs=in_specs, out_specs=out_specs, check_vma=False
    )
```

time: 598 us -> 128 us (0.21); the launches traced: 591 us -> 128 us
  waiting for transfers between devices: 392 us -> 0 us
  other arithmetic: 134 us -> 0 us
  Pallas kernels: 0 us -> 120 us
  matrix products: 37.9 us -> 0 us
  between operations: 14.3 us -> 0.66 us
    all_gather x4 -> x0, waiting for transfers between devices: 265 us -> none  [the longest x2 135 us: prefix(): everything = lax.all_gather(value.astype(jnp.bfloat16), axis)]
    select_n x128 -> x0, other arithmetic: 133 us -> none  [lap(): return jnp.where(reached, new, before)]
    reduce_scatter x2 -> x0, waiting for transfers between devices: 126 us -> none  [the longest x1 126 us: on_device(): lax.psum_scatter(weight_part, 'ctx', scatter_dimension=1, tiled=True)]
    pallas_call x0 -> x1, Pallas kernels: none -> 120 us  [on_device(): pl.pallas_call(kernel, out_shape=(jax.ShapeDtypeStruct((ROWS, cols), BF16...]
    dot_general x15 -> x0, matrix products: 37.9 us -> none  [the longest x1 6.81 us: on_device(): lax.dot_general(full_cot, whole_weight, (((1,), (1,)), ((), ())), preferr...]
  transfers between devices with their start and end apart: 6 -> 0, of which waited for: 5 -> 0; matrix products, arithmetic and copies ran while one was open for 18% -> 0% of each run, Pallas kernels for 0% -> 0%
where the time goes in v1:
time: 128 us
  Pallas kernels  120 us (94%)
  local copies, waits for them, and re-layouts  7.71 us (6%)
    pallas_call x1, Pallas kernels, on_device(): pl.pallas_call(kernel, out_shape=(jax.ShapeDtypeStruct((ROWS, cols), BF16...  120 us
    unnamed x15, local copies, waits for them, and re-layouts  7.13 us

profile of v1, /device:TPU:1, one launch (start us, length us, event | category | flops | bytes accessed | tf_op | source)
XLA Modules:
  0.0 127.9 jit_solution(2821358941371000273)
XLA Ops:
  0.6 0.0 copy-start.4
  0.6 0.7 copy-done.4
  1.3 0.6 reshape.13.g_ref
  1.9 119.5 %shard_map.101 = (bf16[512,1024]{1,0:T(8,128)(2,1)}, bf16[512,512]{1,0:T(8,128)(2,1)}, bf16[512,512]{1,0:T(8,128)(2,1)}, bf16[512,512]{1,0:T(8,128)(2,1)}, f32[64,512]{1,0:T(8,128)}) custom-call(bf16[512,512]{1,0:T(8,128)(2,1)} %q_ref.1, bf16[512,512]{1,0:T(8,128)(2,1)} %k_ref.1, bf16[512,512]{1,0:T(8,128)(2,1)} %v_ref.1, bf16[1,512]{1,0:T(2,128)(2,1)} %reshape.13.g_ref, ...), custom_call_target="tpu_custom_call" | custom-call | tf_op jit(solution)/shard_map/pallas_call | solution.py:410
  121.4 0.0 copy-start.2
  121.4 2.3 %copy.16 = bf16[512,1024]{1,0:T(8,128)(2,1)} copy(bf16[512,1024]{1,0:T(8,128)(2,1)} %get-tuple-element.20) | data formatting | bytes 2097152
  123.8 0.0 copy-done.2
  123.8 0.0 copy-start.1
  123.8 0.8 copy.17
  124.6 0.4 copy-done.1
  125.0 0.0 copy-start
  125.0 0.8 copy.18
  125.8 0.4 copy-done
  126.2 0.0 copy-start.3
  126.2 0.8 copy.19
  127.0 0.2 copy-done.3
  127.2 0.7 copy.20
Async XLA Ops:
  0.6 0.7 copy-start.4
  121.4 2.3 %copy-start.2 = (bf16[512,512]{1,0:T(8,128)(2,1)S(1)}, bf16[512,512]{1,0:T(8,128)(2,1)}, u32[]{:S(2)}) copy-start(bf16[512,512]{1,0:T(8,128)(2,1)} %get-tuple-element.21) | copy-start | bytes 1572868
  123.8 1.2 copy-start.1
  125.0 1.2 copy-start
  126.2 1.0 copy-start.3

commit v2 on v1

v2 whole, which is shorter than its diff:
```python
import jax
import jax.numpy as jnp
from jax import lax
from jax.experimental import pallas as pl
from jax.experimental.pallas import tpu as pltpu
from jax.sharding import PartitionSpec as P

HDIM = 128
HEADS = 4
ROWS = 512
NX, NY, NZ = 4, 4, 8
GROUP = 2 * NZ
SLICE = HEADS * HDIM // GROUP
PIECE = 64
EPS = 1e-06
MESH = pl.DeviceIdType.MESH
F32, BF16 = jnp.float32, jnp.bfloat16


def dot(a, b, ca, cb):
    return lax.dot_general(a, b, (((ca,), (cb,)), ((), ())), preferred_element_type=F32)


def copy_to(src, dst, send_sem, recv_sem, device):
    return pltpu.make_async_remote_copy(
        src_ref=src, dst_ref=dst, send_sem=send_sem, recv_sem=recv_sem,
        device_id=device, device_id_type=MESH,
    )


def head(h):
    return slice(h * HDIM, (h + 1) * HDIM)


class Ring:
    def __init__(self, n, at, step, view, send_sem, recv_sem, device, sent, landed=None):
        self.n, self.at, self.step, self.view = n, at, step, view
        self.sems = send_sem, recv_sem
        self.major, self.minor = device((at + step + n) % n), device((at - step + n) % n)
        self.sent, self.landed = sent, landed

    def send(self, i, src, place, way):
        c = copy_to(src, self.view(place), self.sems[0].at[i], self.sems[1].at[i], way)
        c.start()
        self.sent.append(c)

    def arrive(self, i, place):
        view = self.view(place)
        copy_to(view, view, self.sems[0].at[i], self.sems[1].at[i], self.major).wait_recv()

    def start(self, src=None):
        src = self.view(self.at) if src is None else src
        self.send(0, src, self.at, self.major)
        self.send(self.n // 2, src, self.at, self.minor)
        if self.landed:
            self.landed(self.at)

    def go(self, s):
        n, half = self.n, self.n // 2
        places = [((self.at - self.step * s + n) % n, s - 1, s, self.major, s < half)]
        if s < half:
            places.append(((self.at + self.step * s + n) % n, half + s - 1, half + s, self.minor, s < half - 1))
        for place, came, goes, way, more in places:
            self.arrive(came, place)
            if more:
                self.send(goes, self.view(place), place, way)
            if self.landed:
                self.landed(place)


def kernel(
    q_ref, k_ref, v_ref, g_ref, w_ref, c_ref,
    out_ref, gq_ref, gk_ref, gv_ref, gw_ref,
    wt, wc, ca, state, slices, partial, totals, back, states,
    att, inv, normed, cot_t, gn, ga,
    pair_stage, pair_recv, dsum, ring_stage, ring_recv, last_stage, last_recv,
    ay_send, ay_recv, az_send, az_recv, ac_send, ac_recv,
    bz_send, bz_recv, by_send, by_recv, bc_send, bc_recv,
    pm_send, pm_recv, cz_send, cz_recv, cy_send, cy_recv, cc_send, cc_recv,
    ca_send, ca_recv,
    s1_send, s1_recv, s2_send, s2_recv, s3_send, s3_recv,
    n_send, n_recv, pair_send, pair_rsem,
    ring_send, ring_rsem, last_send, last_rsem,
):
    ctx, x = lax.axis_index("ctx"), lax.axis_index("head")
    y, z, core = ctx // GROUP, (ctx // 2) % NZ, ctx % 2
    g = ctx % GROUP
    me_diag = x == y

    def dev(x, y, z, core):
        return (y * GROUP + z * 2 + core, x)

    step = 1 - 2 * core
    z_major, z_minor = (z + step + NZ) % NZ, (z - step + NZ) % NZ
    x_opp = (x + 2) % NX
    d_major, d_minor = dev(x, y, z_major, core), dev(x, y, z_minor, core)
    sibling = dev(x, y, z, 1 - core)
    sent = []

    def send(*args):
        c = copy_to(*args)
        c.start()
        sent.append(c)

    barrier = pltpu.get_barrier_semaphore()

    def hello(device):
        pl.semaphore_signal(barrier, inc=1, device_id=device, device_id_type=MESH)

    def hello_group(d, carry):
        hello((y * GROUP + (g + d) % GROUP, x))
        return carry

    lax.fori_loop(1, GROUP, hello_group, 0)
    for d in range(1, NY):
        hello(dev(x, (y + d) % NY, z, core))
    hello(dev((x + 1) % NX, y, z, core))
    hello(dev((x + 3) % NX, y, z, core))

    @pl.when(x != y)
    def _():
        hello(dev(y, x, z, core))


    def on_y(j):
        return dev(x, j, z, core)

    def on_z(j):
        return dev(x, y, j, core)

    def on_x(j):
        return dev(j, y, z, core)

    def exchange(view, send_sem, recv_sem):
        def landed(place):
            send(view(place), view(place), send_sem.at[place], recv_sem.at[place], sibling)

        return landed

    def exchanged(n, view, send_sem, recv_sem):
        for i in range(n):
            copy_to(view(i), view(i), send_sem.at[i], recv_sem.at[i], sibling).wait_recv()

    half = PIECE // 2
    low, high = pl.ds(0, half), pl.ds(half, half)
    az_view = lambda i, c=core: wt.at[i, c, :, low]
    by_view = lambda i, c=core: wt.at[:, c, i, high]
    cy_view = lambda i, c=core: wc.at[i, :, c]
    ring_ay = Ring(NY, y, step, lambda i: wt.at[z, core, i, low], ay_send, ay_recv, on_y, sent)
    ring_az = Ring(NZ, z, step, az_view, az_send, az_recv, on_z, sent, exchange(az_view, ac_send, ac_recv))
    ring_bz = Ring(NZ, z, step, lambda i: wt.at[i, core, y, high], bz_send, bz_recv, on_z, sent)
    ring_by = Ring(NY, y, step, by_view, by_send, by_recv, on_y, sent, exchange(by_view, bc_send, bc_recv))
    ring_cz = Ring(NZ, z, step, lambda i: wc.at[y, i, core], cz_send, cz_recv, on_z, sent)
    ring_cy = Ring(NY, y, step, cy_view, cy_send, cy_recv, on_y, sent, exchange(cy_view, cc_send, cc_recv))
    rows = [pl.ds(0, ROWS // 2), pl.ds(ROWS // 2, ROWS // 2)]
    ring_cot = [
        Ring(NX, x, step, lambda i, r=r: ca.at[i, r], ca_send.at[h], ca_recv.at[h], on_x, sent)
        for h, r in enumerate(rows)
    ]
    ring_n = Ring(NX, x, step, lambda i: normed.at[i], n_send, n_recv, on_x, sent)

    def turned():
        @pl.when(x != y)
        def _():
            copy_to(w_ref, wc.at[y, z, core], pm_send.at[0], pm_recv.at[0], sibling).wait_recv()

    def scan_state(way):
        for h in range(HEADS):
            state[way, h * (HDIM // SLICE):(h + 1) * (HDIM // SLICE)] = (
                scan_term(way, h).astype(BF16).reshape(HDIM // SLICE, SLICE, HDIM)
            )

    def scan_start(way):
        if way:
            scan_state(way)

        def go(d, carry):
            to = (g + d) % GROUP
            copy_to(state.at[way, to], slices.at[way, g], s1_send.at[way, d], s1_recv.at[way, g],
                    (y * GROUP + to, x)).start()
            return carry

        lax.fori_loop(1, GROUP, go, 0)
        slices[way, g] = state[way, g]

    def scan_term(way, h):
        if way == 0:
            return dot(k_ref[:, head(h)], v_ref[:, head(h)], 0, 0)
        return dot(q_ref[:, head(h)], ga[:, head(h)], 0, 0)

    def scan_totals(way):
        def arrive(d, carry):
            at = (g + d) % GROUP
            copy_to(slices.at[way, at], slices.at[way, at], s1_send.at[way, d], s1_recv.at[way, at], sibling).wait_recv()
            return carry

        lax.fori_loop(1, GROUP, arrive, 0)
        run = jnp.zeros((SLICE, HDIM), F32)
        for i in (range(GROUP) if way == 0 else range(GROUP - 1, -1, -1)):
            partial[way, i] = run
            run = run + slices[way, i].astype(F32)
        totals[way, y] = run
        for d in range(1, NY):
            send(totals.at[way, y], totals.at[way, y], s2_send.at[way, d], s2_recv.at[way, y],
                 dev(x, (y + d) % NY, z, core))

    def scan_back(way):
        for d in range(1, NY):
            at = (y + d) % NY
            copy_to(totals.at[way, at], totals.at[way, at], s2_send.at[way, d], s2_recv.at[way, at], sibling).wait_recv()
        offset = jnp.zeros((SLICE, HDIM), F32)
        for j in range(NY):
            counts = (j < y) if way == 0 else (j > y)
            offset = offset + jnp.where(counts, totals[way, j], 0.0)
        for i in range(GROUP):
            back[way, i] = (partial[way, i] + offset).astype(BF16)

        def go(d, carry):
            to = (g + d) % GROUP
            copy_to(back.at[way, to], states.at[way, g], s3_send.at[way, d], s3_recv.at[way, g],
                    (y * GROUP + to, x)).start()
            return carry

        lax.fori_loop(1, GROUP, go, 0)
        states[way, g] = back[way, g]

    def scan_end(way):
        def arrive(d, carry):
            at = (g + d) % GROUP
            copy_to(states.at[way, at], states.at[way, at], s3_send.at[way, d], s3_recv.at[way, at], sibling).wait_recv()
            return carry

        lax.fori_loop(1, GROUP, arrive, 0)

    def state_of(way, h):
        n = HDIM // SLICE
        return states[way, h * n:(h + 1) * n].reshape(HDIM, HDIM)


    gain = g_ref[...].astype(F32)
    row = lax.broadcasted_iota(jnp.int32, (ROWS, ROWS), 0)
    col = lax.broadcasted_iota(jnp.int32, (ROWS, ROWS), 1)

    def local_attention(h):
        s = dot(q_ref[:, head(h)], k_ref[:, head(h)], 1, 1)
        m = jnp.where(row >= col, s, 0.0).astype(BF16)
        att[:, head(h)] = dot(m, v_ref[:, head(h)], 1, 0)

    def attend():
        for h in range(HEADS):
            a = att[:, head(h)] + dot(q_ref[:, head(h)], state_of(0, h), 1, 0)
            scale = lax.rsqrt(jnp.mean(a * a, axis=-1, keepdims=True) + EPS)
            a = a * scale
            att[:, head(h)] = a
            inv[h] = scale
            normed[x, :, head(h)] = (a * gain[:, head(h)]).astype(BF16)


    def cot_of(p):
        return c_ref[...] if p == 0 else ca[quarters[p]]

    def pair_go(p):
        cot_t[...] = cot_of(p).T.reshape(NZ, 2, PIECE, ROWS)
        other = cot_t[:, 1 - core].reshape(ROWS, ROWS)
        pair_stage[p] = dot(other, normed[x], 1, 0).astype(BF16).reshape(NZ, PIECE, ROWS)
        send(pair_stage.at[p], pair_recv.at[p], pair_send.at[p], pair_rsem.at[p], sibling)

    def pair_mine(p):
        mine = cot_t[:, core].reshape(ROWS, ROWS)
        dsum[p] = dot(mine, normed[x], 1, 0).reshape(NZ, PIECE, ROWS)

    def pair_end(p):
        copy_to(pair_stage.at[p], pair_recv.at[p], pair_send.at[p], pair_rsem.at[p], sibling).wait_recv()
        dsum[p] = dsum[p] + pair_recv[p].astype(F32)

    def ring_wait(p, i):
        copy_to(ring_stage.at[p, i], ring_recv.at[p, i], ring_send.at[p, i], ring_rsem.at[p, i], sibling).wait_recv()

    def ring_step(p, s):
        at = (z + step * (4 - s) + NZ) % NZ
        term = dsum[p, at]
        if s:
            ring_wait(p, s - 1)
            term = term + ring_recv[p, s - 1].astype(F32)
        ring_stage[p, s] = term.astype(BF16)
        send(ring_stage.at[p, s], ring_recv.at[p, s], ring_send.at[p, s], ring_rsem.at[p, s], d_major)
        if s < 3:
            at = (z - step * (3 - s) + NZ) % NZ
            term = dsum[p, at]
            if s:
                ring_wait(p, 3 + s)
                term = term + ring_recv[p, 3 + s].astype(F32)
            i = 4 + s
            ring_stage[p, i] = term.astype(BF16)
            send(ring_stage.at[p, i], ring_recv.at[p, i], ring_send.at[p, i], ring_rsem.at[p, i], d_minor)

    def ring_end(p):
        ring_wait(p, 3)
        ring_wait(p, 6)
        total = dsum[p, z] + ring_recv[p, 3].astype(F32) + ring_recv[p, 6].astype(F32)
        last_stage[p] = total.astype(BF16)
        a = quarters[p]

        @pl.when(a != y)
        def _():
            copy_to(last_stage.at[p], last_recv.at[y], last_send.at[p], last_rsem.at[y], dev(x, a, z, core)).start()

        @pl.when(a == y)
        def _():
            last_recv[y] = last_stage[p]

    quarters = (x, (x + 3) % NX, (x + 1) % NX, x_opp)

    def gn_part(p):
        w = wt[:, :, quarters[p]].reshape(NZ * 2 * PIECE, ROWS)
        part = dot(cot_of(p), w, 1, 0)
        gn[...] = part if p == 0 else gn[...] + part

    def gradient():
        for h in range(HEADS):
            w = gn[:, head(h)] * gain[:, head(h)]
            a = att[:, head(h)]
            along = jnp.mean(w * a, axis=-1, keepdims=True)
            ga[:, head(h)] = (inv[h] * (w - a * along)).astype(BF16)

    def queries_gradient(h):
        s = dot(ga[:, head(h)], v_ref[:, head(h)], 1, 1)
        m = jnp.where(row >= col, s, 0.0).astype(BF16)
        t = dot(m, k_ref[:, head(h)], 1, 0) + dot(ga[:, head(h)], state_of(0, h), 1, 1)
        gq_ref[:, head(h)] = t.astype(BF16)

    def local_keys_values(h):
        s = dot(v_ref[:, head(h)], ga[:, head(h)], 1, 1)
        m = jnp.where(col >= row, s, 0.0).astype(BF16)
        gn[:, head(h)] = dot(m, q_ref[:, head(h)], 1, 0)
        s = dot(k_ref[:, head(h)], q_ref[:, head(h)], 1, 1)
        m = jnp.where(col >= row, s, 0.0).astype(BF16)
        att[:, head(h)] = dot(m, ga[:, head(h)], 1, 0)

    def finish():
        for h in range(HEADS):
            st = state_of(1, h)
            gk_ref[:, head(h)] = (gn[:, head(h)] + dot(v_ref[:, head(h)], st, 1, 1)).astype(BF16)
            gv_ref[:, head(h)] = (att[:, head(h)] + dot(k_ref[:, head(h)], st, 1, 0)).astype(BF16)


    def layer_out():
        def out_rows(i, carry):
            r = pl.ds(pl.multiple_of(i * 128, 128), 128)
            total = jnp.zeros((128, NZ * 2 * PIECE), F32)
            for a in range(NX):
                total = total + dot(normed[a, r, :], wc[a].reshape(NZ * 2 * PIECE, ROWS), 1, 1)
            out_ref[r, :] = total.astype(BF16)
            return carry

        lax.fori_loop(0, ROWS // 128, out_rows, 0)


    def gw_sum():
        for d in range(1, NY):
            j = (y + d) % NY
            copy_to(last_stage.at[0], last_recv.at[j], last_send.at[0], last_rsem.at[j], sibling).wait_recv()
        gw_ref[...] = (
            (last_recv[0].astype(F32) + last_recv[1].astype(F32))
            + (last_recv[2].astype(F32) + last_recv[3].astype(F32))
        )

    scan_state(0)
    local_attention(0)
    local_attention(1)
    local_attention(2)
    wt[z, core, y] = w_ref[...]

    @pl.when(x == y)
    def _():
        wc[x, z, core] = w_ref[...]

    pl.semaphore_wait(barrier, (GROUP - 1) + (NY - 1) + 3 - me_diag.astype(jnp.int32))

    @pl.when(x != y)
    def _():
        copy_to(w_ref, wc.at[x, z, core], pm_send.at[0], pm_recv.at[0], dev(y, x, z, core)).start()

    ring_cot[0].start(c_ref.at[rows[0]])
    local_attention(3)
    ring_bz.start()
    ring_ay.start()
    scan_start(0)
    ring_cot[1].start(c_ref.at[rows[1]])
    ring_bz.go(1)
    ring_ay.go(1)
    turned()
    ring_cz.start()
    ring_ay.go(2)
    ring_az.start()
    ring_bz.go(2)
    scan_totals(0)
    ring_cz.go(1)
    ring_bz.go(3)
    scan_back(0)
    ring_az.go(1)
    ring_bz.go(4)
    ring_by.start()
    ring_cz.go(2)
    scan_end(0)
    attend()
    ring_cz.go(3)
    pair_go(0)
    pair_mine(0)
    ring_az.go(2)
    ring_by.go(1)
    ring_cz.go(4)
    pair_end(0)
    ring_step(0, 0)
    ring_cot[0].go(1)
    ring_cot[1].go(1)
    pair_go(1)
    pair_mine(1)
    ring_az.go(3)
    ring_by.go(2)
    ring_cy.start()
    ring_step(0, 1)
    pair_end(1)
    ring_step(1, 0)
    exchanged(NY, lambda i: by_view(i, 1 - core), bc_send, bc_recv)
    ring_az.go(4)
    ring_step(0, 2)
    exchanged(NZ, lambda i: az_view(i, 1 - core), ac_send, ac_recv)
    pair_go(2)
    ring_step(1, 1)
    pair_mine(2)
    gn_part(0)
    gn_part(1)
    ring_step(0, 3)
    pair_end(2)
    ring_cot[0].go(2)
    ring_n.start()
    ring_step(2, 0)
    gn_part(2)
    ring_cot[1].go(2)
    pair_go(3)
    pair_mine(3)
    ring_step(1, 2)
    gn_part(3)
    ring_end(0)
    gradient()
    pair_end(3)
    ring_step(3, 0)
    ring_cy.go(1)
    scan_start(1)
    ring_step(2, 1)
    local_keys_values(0)
    ring_step(1, 3)
    local_keys_values(1)
    local_keys_values(2)
    local_keys_values(3)
    queries_gradient(0)
    ring_step(3, 1)
    queries_gradient(1)
    queries_gradient(2)
    queries_gradient(3)
    ring_step(2, 2)
    ring_end(1)
    scan_totals(1)
    ring_cy.go(2)
    ring_step(3, 2)
    ring_n.go(1)
    ring_step(2, 3)
    exchanged(NY, lambda i: cy_view(i, 1 - core), cc_send, cc_recv)
    scan_back(1)
    ring_step(3, 3)
    ring_end(2)
    ring_end(3)
    ring_n.go(2)
    layer_out()
    scan_end(1)
    finish()
    gw_sum()

    for c in sent:
        c.wait_send()

    @pl.when(x != y)
    def _():
        copy_to(w_ref, wc.at[x, z, core], pm_send.at[0], pm_recv.at[0], sibling).wait_send()

    for p in range(NX):
        @pl.when(quarters[p] != y)
        def _():
            copy_to(last_stage.at[p], last_recv.at[y], last_send.at[p], last_rsem.at[y], sibling).wait_send()

    def left(d, carry):
        for way in range(2):
            to = (g + d) % GROUP
            copy_to(state.at[way, to], slices.at[way, g], s1_send.at[way, d], s1_recv.at[way, g], sibling).wait_send()
            copy_to(back.at[way, to], states.at[way, g], s3_send.at[way, d], s3_recv.at[way, g], sibling).wait_send()
        return carry

    lax.fori_loop(1, GROUP, left, 0)


def settle(*refs):
    n = (len(refs) - 1) // 3
    sems = refs[-1]
    come = [pltpu.make_async_copy(refs[i], refs[2 * n + i], sems.at[0, i]) for i in range(n)]
    go = [pltpu.make_async_copy(refs[2 * n + i], refs[n + i], sems.at[1, i]) for i in range(n)]
    for c in come:
        c.start()
    for i in range(n):
        come[i].wait()
        go[i].start()
    for c in go:
        c.wait()


def on_device(queries, keys, values, gain, out_weight, cotangent):
    width = HEADS * HDIM
    cols = NZ * 2 * PIECE
    vmem = pl.BlockSpec(memory_space=pltpu.VMEM)
    dma = pltpu.SemaphoreType.DMA
    outs = pl.pallas_call(
        kernel,
        out_shape=(
            jax.ShapeDtypeStruct((ROWS, cols), BF16),
            jax.ShapeDtypeStruct((ROWS, width), BF16),
            jax.ShapeDtypeStruct((ROWS, width), BF16),
            jax.ShapeDtypeStruct((ROWS, width), BF16),
            jax.ShapeDtypeStruct((PIECE, width), F32),
        ),
        in_specs=[vmem] * 6,
        out_specs=(vmem,) * 5,
        scratch_shapes=[
            pltpu.VMEM((NZ, 2, NY, PIECE, width), BF16),
            pltpu.VMEM((NX, NZ, 2, PIECE, width), BF16),
            pltpu.VMEM((NX, ROWS, cols), BF16),
            pltpu.VMEM((2, GROUP, SLICE, HDIM), BF16),
            pltpu.VMEM((2, GROUP, SLICE, HDIM), BF16),
            pltpu.VMEM((2, GROUP, SLICE, HDIM), F32),
            pltpu.VMEM((2, NY, SLICE, HDIM), F32),
            pltpu.VMEM((2, GROUP, SLICE, HDIM), BF16),
            pltpu.VMEM((2, GROUP, SLICE, HDIM), BF16),
            pltpu.VMEM((ROWS, width), F32),
            pltpu.VMEM((HEADS, ROWS, 1), F32),
            pltpu.VMEM((NX, ROWS, width), BF16),
            pltpu.VMEM((NZ, 2, PIECE, ROWS), BF16),
            pltpu.VMEM((ROWS, width), F32),
            pltpu.VMEM((ROWS, width), BF16),
            pltpu.VMEM((NX, NZ, PIECE, width), BF16),
            pltpu.VMEM((NX, NZ, PIECE, width), BF16),
            pltpu.VMEM((NX, NZ, PIECE, width), F32),
            pltpu.VMEM((NX, 7, PIECE, width), BF16),
            pltpu.VMEM((NX, 7, PIECE, width), BF16),
            pltpu.VMEM((NX, PIECE, width), BF16),
            pltpu.VMEM((NY, PIECE, width), BF16),
            dma((3,)), dma((3,)), dma((7,)), dma((7,)), dma((NZ,)), dma((NZ,)),
            dma((7,)), dma((7,)), dma((3,)), dma((3,)), dma((NY,)), dma((NY,)),
            dma((1,)), dma((1,)), dma((7,)), dma((7,)), dma((3,)), dma((3,)), dma((NY,)), dma((NY,)),
            dma((2, 3)), dma((2, 3)),
            dma((2, GROUP)), dma((2, GROUP)), dma((2, NY)), dma((2, NY)), dma((2, GROUP)), dma((2, GROUP)),
            dma((3,)), dma((3,)), dma((NX,)), dma((NX,)),
            dma((NX, 7)), dma((NX, 7)), dma((NX,)), dma((NY,)),
        ],
        compiler_params=pltpu.CompilerParams(
            collective_id=0, has_side_effects=True, vmem_limit_bytes=56 * 1024 * 1024
        ),
    )(queries, keys, values, gain.reshape(1, width), out_weight.T, cotangent)
    anywhere = pl.BlockSpec(memory_space=pl.ANY)
    outs = pl.pallas_call(
        settle,
        out_shape=tuple(jax.ShapeDtypeStruct(o.shape, o.dtype) for o in outs),
        in_specs=[anywhere] * len(outs),
        out_specs=(anywhere,) * len(outs),
        scratch_shapes=[pltpu.VMEM(o.shape, o.dtype) for o in outs] + [dma((2, len(outs)))],
    )(*outs)
    return outs[:4] + (outs[4].T,)


def solution(mesh):
    in_specs = (
        P("ctx", "head"),
        P("ctx", "head"),
        P("ctx", "head"),
        P("head"),
        P("head", "ctx"),
        P("ctx", "head"),
    )
    out_specs = (
        P("ctx", "head"),
        P("ctx", "head"),
        P("ctx", "head"),
        P("ctx", "head"),
        P("head", "ctx"),
    )
    return jax.shard_map(
        on_device, mesh=mesh, in_specs=in_specs, out_specs=out_specs, check_vma=False
    )
```

time: 128 us -> 91.2 us (0.71)
  the two profiles are of different devices: /device:TPU:1 before, /device:TPU:8 now
where the time goes in v2:
time: 91.2 us; the launch traced here: 91 us
  Pallas kernels  88.9 us (97%)
  local copies, waits for them, and re-layouts  1.25 us (1%)
    pallas_call x1, Pallas kernels, on_device(): pl.pallas_call(kernel, out_shape=(jax.ShapeDtypeStruct((ROWS, cols), BF16...  86.1 us
    pallas_call x1, Pallas kernels, on_device(): pl.pallas_call(settle, out_shape=tuple((jax.ShapeDtypeStruct(o.shape, o.d...  2.83 us

profile of v2, /device:TPU:8, one launch (start us, length us, event | category | flops | bytes accessed | tf_op | source)
XLA Modules:
  0.0 91.0 jit_solution(13502041187877792770)
XLA Ops:
  0.6 0.0 copy-start
  0.6 0.7 copy-done
  1.3 0.6 reshape.13.g_ref
  1.9 86.1 %shard_map.101 = (bf16[512,1024]{1,0:T(8,128)(2,1)}, bf16[512,512]{1,0:T(8,128)(2,1)}, bf16[512,512]{1,0:T(8,128)(2,1)}, bf16[512,512]{1,0:T(8,128)(2,1)}, f32[64,512]{1,0:T(8,128)}) custom-call(bf16[512,512]{1,0:T(8,128)(2,1)} %q_ref.1, bf16[512,512]{1,0:T(8,128)(2,1)} %k_ref.1, bf16[512,512]{1,0:T(8,128)(2,1)} %v_ref.1, bf16[1,512]{1,0:T(2,128)(2,1)} %reshape.13.g_ref, ...), custom_call_target="tpu_custom_call" | custom-call | tf_op jit(solution)/shard_map/pallas_call | solution.py:521
  88.0 2.8 %shard_map.102 = (bf16[512,1024]{1,0:T(8,128)(2,1)}, bf16[512,512]{1,0:T(8,128)(2,1)}, bf16[512,512]{1,0:T(8,128)(2,1)}, bf16[512,512]{1,0:T(8,128)(2,1)}, f32[64,512]{1,0:T(8,128)}) custom-call(bf16[512,1024]{1,0:T(8,128)(2,1)} %get-tuple-element.15.refs_0_, bf16[512,512]{1,0:T(8,128)(2,1)} %get-tuple-element.16.refs_1_, ...), custom_call_target="tpu_custom_call" | custom-call | tf_op jit(solution)/shard_map/pallas_call | solution.py:568
Async XLA Ops:
  0.6 0.7 copy-start

commit v3 on v2

--- a/solution.py
+++ b/solution.py
@@ -69,12 +69,12 @@
 
 
 def kernel(
-    q_ref, k_ref, v_ref, g_ref, w_ref, c_ref,
+    q_in, k_in, v_in, g_ref, w_ref, c_in,
     out_ref, gq_ref, gk_ref, gv_ref, gw_ref,
-    wt, wc, ca, state, slices, partial, totals, back, states,
-    att, inv, normed, cot_t, gn, ga,
+    q_ref, k_ref, v_ref, c_ref, wt, wc, ca, state, slices, partial, totals, back, states,
+    att, inv, normed, cot_t, gn, ga, acc,
     pair_stage, pair_recv, dsum, ring_stage, ring_recv, last_stage, last_recv,
-    ay_send, ay_recv, az_send, az_recv, ac_send, ac_recv,
+    in_sem, ay_send, ay_recv, az_send, az_recv, ac_send, ac_recv,
     bz_send, bz_recv, by_send, by_recv, bc_send, bc_recv,
     pm_send, pm_recv, cz_send, cz_recv, cy_send, cy_recv, cc_send, cc_recv,
     ca_send, ca_recv,
@@ -121,6 +121,15 @@
     def _():
         hello(dev(y, x, z, core))
 
+
+    inputs = [
+        pltpu.make_async_copy(there, here, in_sem.at[i])
+        for i, (there, here) in enumerate(
+            ((k_in, k_ref), (v_in, v_ref), (q_in, q_ref), (w_ref, wt.at[z, core, y]), (c_in, c_ref))
+        )
+    ]
+    for c in inputs:
+        c.start()
 
     def on_y(j):
         return dev(x, j, z, core)
@@ -237,7 +246,7 @@
         return states[way, h * n:(h + 1) * n].reshape(HDIM, HDIM)
 
 
-    gain = g_ref[...].astype(F32)
+    gain = g_ref[...].astype(F32).reshape(1, HEADS * HDIM)
     row = lax.broadcasted_iota(jnp.int32, (ROWS, ROWS), 0)
     col = lax.broadcasted_iota(jnp.int32, (ROWS, ROWS), 1)
 
@@ -344,17 +353,15 @@
             gv_ref[:, head(h)] = (att[:, head(h)] + dot(k_ref[:, head(h)], st, 1, 0)).astype(BF16)
 
 
-    def layer_out():
-        def out_rows(i, carry):
-            r = pl.ds(pl.multiple_of(i * 128, 128), 128)
-            total = jnp.zeros((128, NZ * 2 * PIECE), F32)
-            for a in range(NX):
-                total = total + dot(normed[a, r, :], wc[a].reshape(NZ * 2 * PIECE, ROWS), 1, 1)
-            out_ref[r, :] = total.astype(BF16)
-            return carry
-
-        lax.fori_loop(0, ROWS // 128, out_rows, 0)
-
+    def out_part(p):
+        a = quarters[p]
+        part = dot(normed[a], wc[a].reshape(NZ * 2 * PIECE, ROWS), 1, 1)
+        if p:
+            part = part + acc[...]
+        if p < NX - 1:
+            acc[...] = part
+        else:
+            out_ref[...] = part.astype(BF16)
 
     def gw_sum():
         for d in range(1, NY):
@@ -365,15 +372,20 @@
             + (last_recv[2].astype(F32) + last_recv[3].astype(F32))
         )
 
+    for c in inputs[:2]:
+        c.wait()
     scan_state(0)
+    inputs[2].wait()
     local_attention(0)
     local_attention(1)
     local_attention(2)
-    wt[z, core, y] = w_ref[...]
+    inputs[3].wait()
 
     @pl.when(x == y)
     def _():
-        wc[x, z, core] = w_ref[...]
+        turn = pltpu.make_async_copy(w_ref, wc.at[x, z, core], in_sem.at[5])
+        turn.start()
+        turn.wait()
 
     pl.semaphore_wait(barrier, (GROUP - 1) + (NY - 1) + 3 - me_diag.astype(jnp.int32))
 
@@ -381,98 +393,102 @@
     def _():
         copy_to(w_ref, wc.at[x, z, core], pm_send.at[0], pm_recv.at[0], dev(y, x, z, core)).start()
 
-    ring_cot[0].start(c_ref.at[rows[0]])
+    ring_cot[0].start(c_in.at[rows[0]])
+    ring_bz.start()
+    scan_start(0)
+    ring_cot[1].start(c_in.at[rows[1]])
+    ring_ay.start()
     local_attention(3)
-    ring_bz.start()
-    ring_ay.start()
-    scan_start(0)
-    ring_cot[1].start(c_ref.at[rows[1]])
     ring_bz.go(1)
     ring_ay.go(1)
     turned()
     ring_cz.start()
+    ring_bz.go(2)
     ring_ay.go(2)
     ring_az.start()
-    ring_bz.go(2)
     scan_totals(0)
     ring_cz.go(1)
     ring_bz.go(3)
     scan_back(0)
     ring_az.go(1)
+    ring_cot[0].go(1)
+    ring_cz.go(2)
     ring_bz.go(4)
     ring_by.start()
-    ring_cz.go(2)
     scan_end(0)
     attend()
-    ring_cz.go(3)
+    inputs[4].wait()
     pair_go(0)
     pair_mine(0)
+    ring_cz.go(3)
     ring_az.go(2)
+    pair_end(0)
+    ring_step(0, 0)
     ring_by.go(1)
     ring_cz.go(4)
-    pair_end(0)
-    ring_step(0, 0)
-    ring_cot[0].go(1)
     ring_cot[1].go(1)
-    pair_go(1)
-    pair_mine(1)
+    pair_go(2)
     ring_az.go(3)
+    pair_mine(2)
     ring_by.go(2)
     ring_cy.start()
+    pair_go(1)
     ring_step(0, 1)
+    pair_mine(1)
+    pair_end(2)
+    exchanged(NY, lambda i: by_view(i, 1 - core), bc_send, bc_recv)
+    ring_step(2, 0)
+    ring_az.go(4)
     pair_end(1)
     ring_step(1, 0)
-    exchanged(NY, lambda i: by_view(i, 1 - core), bc_send, bc_recv)
-    ring_az.go(4)
-    ring_step(0, 2)
+    ring_cot[0].go(2)
+    ring_n.start()
     exchanged(NZ, lambda i: az_view(i, 1 - core), ac_send, ac_recv)
-    pair_go(2)
-    ring_step(1, 1)
-    pair_mine(2)
     gn_part(0)
     gn_part(1)
+    ring_step(0, 2)
+    gn_part(2)
+    ring_step(2, 1)
+    ring_step(1, 1)
     ring_step(0, 3)
-    pair_end(2)
-    ring_cot[0].go(2)
-    ring_n.start()
-    ring_step(2, 0)
-    gn_part(2)
     ring_cot[1].go(2)
     pair_go(3)
     pair_mine(3)
-    ring_step(1, 2)
+    ring_step(2, 2)
     gn_part(3)
-    ring_end(0)
     gradient()
     pair_end(3)
     ring_step(3, 0)
+    ring_end(0)
+    scan_start(1)
+    queries_gradient(0)
     ring_cy.go(1)
-    scan_start(1)
-    ring_step(2, 1)
-    local_keys_values(0)
-    ring_step(1, 3)
-    local_keys_values(1)
-    local_keys_values(2)
-    local_keys_values(3)
-    queries_gradient(0)
-    ring_step(3, 1)
     queries_gradient(1)
     queries_gradient(2)
     queries_gradient(3)
-    ring_step(2, 2)
+    ring_step(1, 2)
+    local_keys_values(0)
+    local_keys_values(1)
+    ring_step(3, 1)
+    local_keys_values(2)
+    local_keys_values(3)
+    ring_step(2, 3)
+    ring_step(1, 3)
+    scan_totals(1)
+    ring_step(3, 2)
+    ring_end(2)
+    ring_n.go(1)
     ring_end(1)
-    scan_totals(1)
     ring_cy.go(2)
-    ring_step(3, 2)
-    ring_n.go(1)
-    ring_step(2, 3)
+    ring_step(3, 3)
+    scan_back(1)
     exchanged(NY, lambda i: cy_view(i, 1 - core), cc_send, cc_recv)
-    scan_back(1)
-    ring_step(3, 3)
-    ring_end(2)
+    out_part(0)
+    out_part(1)
+    out_part(2)
     ring_end(3)
     ring_n.go(2)
-    layer_out()
+    out_part(3)
     scan_end(1)
     finish()
     gw_sum()
@@ -500,16 +516,11 @@
 
 
 def settle(*refs):
-    n = (len(refs) - 1) // 3
-    sems = refs[-1]
-    come = [pltpu.make_async_copy(refs[i], refs[2 * n + i], sems.at[0, i]) for i in range(n)]
-    go = [pltpu.make_async_copy(refs[2 * n + i], refs[n + i], sems.at[1, i]) for i in range(n)]
-    for c in come:
+    n = (len(refs) - 1) // 2
+    copies = [pltpu.make_async_copy(refs[i], refs[n + i], refs[-1].at[i]) for i in range(n)]
+    for c in copies:
         c.start()
-    for i in range(n):
-        come[i].wait()
-        go[i].start()
-    for c in go:
+    for c in copies:
         c.wait()
 
 
@@ -517,19 +528,25 @@
     width = HEADS * HDIM
     cols = NZ * 2 * PIECE
     vmem = pl.BlockSpec(memory_space=pltpu.VMEM)
+    anywhere = pl.BlockSpec(memory_space=pl.ANY)
+    hbm = pl.BlockSpec(memory_space=pltpu.HBM)
     dma = pltpu.SemaphoreType.DMA
     outs = pl.pallas_call(
         kernel,
         out_shape=(
-            jax.ShapeDtypeStruct((ROWS, cols), BF16),
-            jax.ShapeDtypeStruct((ROWS, width), BF16),
-            jax.ShapeDtypeStruct((ROWS, width), BF16),
-            jax.ShapeDtypeStruct((ROWS, width), BF16),
-            jax.ShapeDtypeStruct((PIECE, width), F32),
+            pltpu.VMEM((ROWS, cols), BF16),
+            pltpu.VMEM((ROWS, width), BF16),
+            pltpu.VMEM((ROWS, width), BF16),
+            pltpu.VMEM((ROWS, width), BF16),
+            pltpu.VMEM((PIECE, width), F32),
         ),
-        in_specs=[vmem] * 6,
+        in_specs=[hbm, hbm, hbm, vmem, hbm, hbm],
         out_specs=(vmem,) * 5,
         scratch_shapes=[
+            pltpu.VMEM((ROWS, width), BF16),
+            pltpu.VMEM((ROWS, width), BF16),
+            pltpu.VMEM((ROWS, width), BF16),
+            pltpu.VMEM((ROWS, cols), BF16),
             pltpu.VMEM((NZ, 2, NY, PIECE, width), BF16),
             pltpu.VMEM((NX, NZ, 2, PIECE, width), BF16),
             pltpu.VMEM((NX, ROWS, cols), BF16),
@@ -545,6 +562,7 @@
             pltpu.VMEM((NZ, 2, PIECE, ROWS), BF16),
             pltpu.VMEM((ROWS, width), F32),
             pltpu.VMEM((ROWS, width), BF16),
+            pltpu.VMEM((ROWS, cols), F32),
             pltpu.VMEM((NX, NZ, PIECE, width), BF16),
             pltpu.VMEM((NX, NZ, PIECE, width), BF16),
             pltpu.VMEM((NX, NZ, PIECE, width), F32),
@@ -552,6 +570,7 @@
             pltpu.VMEM((NX, 7, PIECE, width), BF16),
             pltpu.VMEM((NX, PIECE, width), BF16),
             pltpu.VMEM((NY, PIECE, width), BF16),
+            dma((6,)),
             dma((3,)), dma((3,)), dma((7,)), dma((7,)), dma((NZ,)), dma((NZ,)),
             dma((7,)), dma((7,)), dma((3,)), dma((3,)), dma((NY,)), dma((NY,)),
             dma((1,)), dma((1,)), dma((7,)), dma((7,)), dma((3,)), dma((3,)), dma((NY,)), dma((NY,)),
@@ -561,16 +580,17 @@
             dma((NX, 7)), dma((NX, 7)), dma((NX,)), dma((NY,)),
         ],
         compiler_params=pltpu.CompilerParams(
-            collective_id=0, has_side_effects=True, vmem_limit_bytes=56 * 1024 * 1024
+            collective_id=0, has_side_effects=True, vmem_limit_bytes=60 * 1024 * 1024
         ),
-    )(queries, keys, values, gain.reshape(1, width), out_weight.T, cotangent)
-    anywhere = pl.BlockSpec(memory_space=pl.ANY)
+    )(queries, keys, values, gain, out_weight.T, cotangent)
+    outs = [pltpu.with_memory_space_constraint(o, pltpu.VMEM) for o in outs]
     outs = pl.pallas_call(
         settle,
         out_shape=tuple(jax.ShapeDtypeStruct(o.shape, o.dtype) for o in outs),
-        in_specs=[anywhere] * len(outs),
+        in_specs=[vmem] * len(outs),
         out_specs=(anywhere,) * len(outs),
-        scratch_shapes=[pltpu.VMEM(o.shape, o.dtype) for o in outs] + [dma((2, len(outs)))],
+        scratch_shapes=[dma((len(outs),))],
+        compiler_params=pltpu.CompilerParams(vmem_limit_bytes=1024 * 1024),
     )(*outs)
     return outs[:4] + (outs[4].T,)
 

time: 91.2 us -> 83 us (0.910)
  the two profiles are of different devices: /device:TPU:8 before, /device:TPU:1 now
where the time goes in v3:
time: 83 us; the launch traced here: 82.8 us
  Pallas kernels  82 us (99%)
    pallas_call x1, Pallas kernels, on_device(): pl.pallas_call(kernel, out_shape=(pltpu.VMEM((ROWS, cols), BF16), pltpu.V...  80.4 us

profile of v3, /device:TPU:1, one launch (start us, length us, event | category | flops | bytes accessed | tf_op | source)
XLA Modules:
  0.0 82.8 jit_solution(11078229291438899401)
XLA Ops:
  0.6 80.4 %shard_map.101 = (bf16[512,1024]{1,0:T(8,128)(2,1)S(1)}, bf16[512,512]{1,0:T(8,128)(2,1)S(1)}, bf16[512,512]{1,0:T(8,128)(2,1)S(1)}, bf16[512,512]{1,0:T(8,128)(2,1)S(1)}, f32[64,512]{1,0:T(8,128)S(1)}) custom-call(bf16[512,512]{1,0:T(8,128)(2,1)} %q_in.1, bf16[512,512]{1,0:T(8,128)(2,1)} %k_in.1, bf16[512,512]{1,0:T(8,128)(2,1)} %v_in.1, ...), custom_call_target="tpu_custom_call" | custom-call | tf_op jit(solution)/shard_map/pallas_call | solution.py:534
  81.1 1.6 %shard_map.102 = (bf16[512,1024]{1,0:T(8,128)(2,1)}, bf16[512,512]{1,0:T(8,128)(2,1)}, bf16[512,512]{1,0:T(8,128)(2,1)}, bf16[512,512]{1,0:T(8,128)(2,1)}, f32[64,512]{1,0:T(8,128)}) custom-call(bf16[512,1024]{1,0:T(8,128)(2,1)S(1)} %get-tuple-element.15.refs_0_, bf16[512,512]{1,0:T(8,128)(2,1)S(1)} %get-tuple-element.16.refs_1_, ...), custom_call_target="tpu_custom_call" | custom-call | tf_op jit(solution)/shard_map/pallas_call | solution.py:587

commit v4 on v3

--- a/solution.py
+++ b/solution.py
@@ -396,20 +396,20 @@
     ring_cot[0].start(c_in.at[rows[0]])
     ring_bz.start()
     scan_start(0)
-    ring_cot[1].start(c_in.at[rows[1]])
     ring_ay.start()
     local_attention(3)
+    ring_cot[1].start(c_in.at[rows[1]])
     ring_bz.go(1)
     ring_ay.go(1)
     turned()
     ring_cz.start()
+    scan_totals(0)
     ring_bz.go(2)
     ring_ay.go(2)
     ring_az.start()
-    scan_totals(0)
     ring_cz.go(1)
+    scan_back(0)
     ring_bz.go(3)
-    scan_back(0)
     ring_az.go(1)
     ring_cot[0].go(1)
     ring_cz.go(2)
@@ -417,73 +417,73 @@
     ring_by.start()
     scan_end(0)
     attend()
+    ring_az.go(2)
     inputs[4].wait()
     pair_go(0)
     pair_mine(0)
     ring_cz.go(3)
-    ring_az.go(2)
     pair_end(0)
     ring_step(0, 0)
     ring_by.go(1)
+    ring_az.go(3)
+    ring_cot[1].go(1)
+    pair_go(1)
+    pair_mine(1)
     ring_cz.go(4)
-    ring_cot[1].go(1)
-    pair_go(2)
-    ring_az.go(3)
-    pair_mine(2)
-    ring_by.go(2)
     ring_cy.start()
-    pair_go(1)
     ring_step(0, 1)
-    pair_mine(1)
-    pair_end(2)
-    exchanged(NY, lambda i: by_view(i, 1 - core), bc_send, bc_recv)
-    ring_step(2, 0)
-    ring_az.go(4)
     pair_end(1)
     ring_step(1, 0)
+    ring_az.go(4)
+    ring_by.go(2)
+    exchanged(NZ, lambda i: az_view(i, 1 - core), ac_send, ac_recv)
+    pair_go(2)
     ring_cot[0].go(2)
+    exchanged(NY, lambda i: by_view(i, 1 - core), bc_send, bc_recv)
+    ring_step(0, 2)
+    gn_part(0)
+    ring_step(1, 1)
+    pair_mine(2)
+    pair_end(2)
+    ring_step(2, 0)
+    gn_part(1)
     ring_n.start()
-    exchanged(NZ, lambda i: az_view(i, 1 - core), ac_send, ac_recv)
-    gn_part(0)
-    gn_part(1)
-    ring_step(0, 2)
     gn_part(2)
-    ring_step(2, 1)
-    ring_step(1, 1)
     ring_step(0, 3)
     ring_cot[1].go(2)
     pair_go(3)
+    ring_step(1, 2)
+    gn_part(3)
+    ring_step(2, 1)
     pair_mine(3)
-    ring_step(2, 2)
-    gn_part(3)
-    gradient()
     pair_end(3)
     ring_step(3, 0)
-    ring_end(0)
+    gradient()
+    ring_cy.go(1)
     scan_start(1)
     queries_gradient(0)
-    ring_cy.go(1)
     queries_gradient(1)
     queries_gradient(2)
-    queries_gradient(3)
-    ring_step(1, 2)
+    ring_step(2, 2)
     local_keys_values(0)
+    ring_step(3, 1)
+    ring_end(0)
+    ring_step(1, 3)
     local_keys_values(1)
-    ring_step(3, 1)
     local_keys_values(2)
     local_keys_values(3)
     ring_step(2, 3)
-    ring_step(1, 3)
     scan_totals(1)
+    ring_n.go(1)
     ring_step(3, 2)
+    ring_cy.go(2)
+    queries_gradient(3)
     ring_end(2)
-    ring_n.go(1)
-    ring_end(1)
-    ring_cy.go(2)
-    ring_step(3, 3)
-    scan_back(1)
     exchanged(NY, lambda i: cy_view(i, 1 - core), cc_send, cc_recv)
     out_part(0)
+    ring_step(3, 3)
+    ring_end(1)
+    scan_back(1)
     out_part(1)
     out_part(2)
     ring_end(3)

time: 83 us -> 80 us (0.964)
  Pallas kernels: 82 us -> 78.4 us
    pallas_call x1, Pallas kernels: 80.4 us -> 76.8 us  [on_device(): pl.pallas_call(kernel, out_shape=(pltpu.VMEM((ROWS, cols), BF16), pltpu.V...]
where the time goes in v4:
time: 80 us; the launch traced here: 79.2 us
  Pallas kernels  78.4 us (98%)
  between operations  0.8 us (1%)
    pallas_call x1, Pallas kernels, on_device(): pl.pallas_call(kernel, out_shape=(pltpu.VMEM((ROWS, cols), BF16), pltpu.V...  76.8 us

profile of v4, /device:TPU:1, one launch (start us, length us, event | category | flops | bytes accessed | tf_op | source)
XLA Modules:
  0.0 79.2 jit_solution(7368351685245247241)
XLA Ops:
  0.6 76.8 %shard_map.101 = (bf16[512,1024]{1,0:T(8,128)(2,1)S(1)}, bf16[512,512]{1,0:T(8,128)(2,1)S(1)}, bf16[512,512]{1,0:T(8,128)(2,1)S(1)}, bf16[512,512]{1,0:T(8,128)(2,1)S(1)}, f32[64,512]{1,0:T(8,128)S(1)}) custom-call(bf16[512,512]{1,0:T(8,128)(2,1)} %q_in.1, bf16[512,512]{1,0:T(8,128)(2,1)} %k_in.1, bf16[512,512]{1,0:T(8,128)(2,1)} %v_in.1, ...), custom_call_target="tpu_custom_call" | custom-call | tf_op jit(solution)/shard_map/pallas_call | solution.py:534
  77.5 1.6 %shard_map.102 = (bf16[512,1024]{1,0:T(8,128)(2,1)}, bf16[512,512]{1,0:T(8,128)(2,1)}, bf16[512,512]{1,0:T(8,128)(2,1)}, bf16[512,512]{1,0:T(8,128)(2,1)}, f32[64,512]{1,0:T(8,128)}) custom-call(bf16[512,1024]{1,0:T(8,128)(2,1)S(1)} %get-tuple-element.15.refs_0_, bf16[512,512]{1,0:T(8,128)(2,1)S(1)} %get-tuple-element.16.refs_1_, ...), custom_call_target="tpu_custom_call" | custom-call | tf_op jit(solution)/shard_map/pallas_call | solution.py:587

commit v5 on v4

--- a/solution.py
+++ b/solution.py
@@ -379,6 +379,7 @@
     local_attention(0)
     local_attention(1)
     local_attention(2)
+    local_attention(3)
     inputs[3].wait()
 
     @pl.when(x == y)
@@ -397,7 +398,6 @@
     ring_bz.start()
     scan_start(0)
     ring_ay.start()
-    local_attention(3)
     ring_cot[1].start(c_in.at[rows[1]])
     ring_bz.go(1)
     ring_ay.go(1)

time: 80 us -> 80.1 us (level)
  no operation moved by 1% of the time
where the time goes in v5:
time: 80.1 us; the launch traced here: 80 us
  Pallas kernels  79.2 us (99%)
    pallas_call x1, Pallas kernels, on_device(): pl.pallas_call(kernel, out_shape=(pltpu.VMEM((ROWS, cols), BF16), pltpu.V...  77.6 us

profile of v5, /device:TPU:1, one launch (start us, length us, event | category | flops | bytes accessed | tf_op | source)
XLA Modules:
  0.0 80.0 jit_solution(18239865984329242419)
XLA Ops:
  0.6 77.6 %shard_map.101 = (bf16[512,1024]{1,0:T(8,128)(2,1)S(1)}, bf16[512,512]{1,0:T(8,128)(2,1)S(1)}, bf16[512,512]{1,0:T(8,128)(2,1)S(1)}, bf16[512,512]{1,0:T(8,128)(2,1)S(1)}, f32[64,512]{1,0:T(8,128)S(1)}) custom-call(bf16[512,512]{1,0:T(8,128)(2,1)} %q_in.1, bf16[512,512]{1,0:T(8,128)(2,1)} %k_in.1, bf16[512,512]{1,0:T(8,128)(2,1)} %v_in.1, ...), custom_call_target="tpu_custom_call" | custom-call | tf_op jit(solution)/shard_map/pallas_call | solution.py:534
  78.2 1.6 %shard_map.102 = (bf16[512,1024]{1,0:T(8,128)(2,1)}, bf16[512,512]{1,0:T(8,128)(2,1)}, bf16[512,512]{1,0:T(8,128)(2,1)}, bf16[512,512]{1,0:T(8,128)(2,1)}, f32[64,512]{1,0:T(8,128)}) custom-call(bf16[512,1024]{1,0:T(8,128)(2,1)S(1)} %get-tuple-element.15.refs_0_, bf16[512,512]{1,0:T(8,128)(2,1)S(1)} %get-tuple-element.16.refs_1_, ...), custom_call_target="tpu_custom_call" | custom-call | tf_op jit(solution)/shard_map/pallas_call | solution.py:587
